TPU v7x, 32 devices: a whole 2x2x4 slice. The times are simulated.
32 devices in a mesh: grp: 2 (over x), vir: 16 (over z, y, core).
Axes of the slice: x: 2, y: 2, z: 4, core: 2. Of those that a mesh axis runs over, the one named last changes fastest.
Arguments:
- amplitudes: bfloat16 [32, 1024, 1024], P(('grp', 'vir')), parts along dimension 0, may hold values from -6 to 6
- couplings: bfloat16 [4096, 16, 2048], P(('grp', 'vir')), parts along dimension 0, may hold values from -0.125 to 0.125
- occ_irrep: int32 [32], P('grp'), parts along dimension 0, may hold values from 0 to 7
- pair_irrep: int32 [1], replicated, may hold values from 0 to 7
- j_irrep: int32 [2], replicated, may hold values from 0 to 7
- block_sizes: int32 [16], P('grp'), parts along dimension 0, may hold values from 1 to 256, 1024 in all
- owner: int32 [512, 1], P('grp'), parts along dimension 0, may hold values from 0 to 15; in each aligned block of 256 rows (0 to 255, 256 to 511, ...) at most 32 rows name the same one
Outputs:
- cycle: float32 [2048, 2048], P(('grp', 'vir')), parts along dimension 0
There are 2 independent parts, one for each index of `grp`. A program takes and returns all parts, laid end to end along the dimension named above; an argument that names none is the same for every part. Nothing has to cross between parts.
Inputs may be any that keep to these rules, and one draw needn't show every extreme that they name: `block_sizes`: the eight blocks are consecutive in virtual order and sum to 1024; the largest holds exactly 256 virtuals. `owner`: no device owns more than 32 blocks, and some device owns exactly 32.
All inputs are finite; a program needn't handle non-finite values.
Results may differ from a plain program's by a relative error of at most 0.0003.
Values may be sent and summed in bfloat16 or wider, within the bound.
No kernel may reach another device: no remote copies, remote signals or barrier semaphores. Data moves between devices by JAX's collectives and lax.ppermute only.
A program may use at most 128 MiB of HBM per device.

v0:
```python
import functools

import jax
import jax.numpy as jnp
from jax import lax
from jax.experimental import pallas as pl
from jax.experimental.pallas import tpu as pltpu
from jax.sharding import PartitionSpec as P

BS = 4
MOST = 256
LIMIT = 24 * 1024 * 1024
F32, BF16, I32, I16 = jnp.float32, jnp.bfloat16, jnp.int32, jnp.int16
TOP = 32767.0
STEPS = 256.0
SMALL = 2.0**-126
HALF = MOST // 2
ALIGN = 16
PAD = 16


def irrep_of(index, sizes):
    label = jnp.zeros_like(index)
    end = jnp.int32(0)
    for h in range(sizes.shape[0] - 1):
        end = end + sizes[h]
        label = jnp.where(index >= end, h + 1, label)
    return label


def iota(shape, dim):
    return lax.broadcasted_iota(I32, shape, dim)


def column_keys(columns, sizes, j_irrep):
    count = j_irrep.shape[0]
    column = iota((1, columns), 1)
    j = column % count
    j_label = jnp.zeros_like(column)
    for i in range(count):
        j_label = jnp.where(j == i, j_irrep[i], j_label)
    return irrep_of(column // count, sizes) ^ j_label


def block_place(owner_row, rows):
    blocks = owner_row.shape[1]
    first, second = iota((blocks, blocks), 0), iota((blocks, blocks), 1)
    owner_col = jnp.sum(jnp.where(first == second, owner_row, 0), axis=1, keepdims=True)
    earlier = (owner_col == owner_row) & (first < second)
    rank = jnp.sum(earlier.astype(I32), axis=0, keepdims=True)
    return owner_row * rows + rank * BS


def virtual_place(place, virtuals):
    blocks = place.shape[1]
    e, block = iota((virtuals, blocks), 0), iota((virtuals, blocks), 1)
    start = jnp.sum(jnp.where(e // BS == block, place, 0), axis=1, keepdims=True)
    return start + iota((virtuals, 1), 0) % BS


def wide_flags(partner, sizes):
    wide = jnp.zeros_like(partner)
    for h in range(sizes.shape[0]):
        wide = jnp.where(partner == h, (sizes[h] > HALF).astype(I32), wide)
    return wide


def wide_block(block, wanted, sizes):
    wide = jnp.zeros_like(block ^ wanted)
    for r in range(BS):
        wide = wide | wide_flags(irrep_of(block * BS + r, sizes) ^ wanted, sizes)
    return wide


def slots_needed(wide, owned):
    return wide + (owned - wide + 1) // 2


def slots_of(wide, rank, rank_wide, count_wide):
    rank_narrow = rank - rank_wide
    slot = jnp.where(wide == 1, rank_wide, count_wide + rank_narrow // 2)
    return slot, jnp.where(wide == 1, 0, 1 + rank_narrow % 2)


def pack_kernel(
    rows_out,
    classes,
    sizes_hbm,
    occ_hbm,
    pair,
    owner_hbm,
    t_hbm,
    *refs,
):
    outs, choice = refs[: len(classes)], refs[len(classes)]
    sizes, occ, owner_row, t_vmem, folds, filled, out, in_sems, out_sems = refs[len(classes) + 1 :]
    virtuals = t_hbm.shape[1]
    blocks = owner_row.shape[1]
    chips = outs[0].shape[0] // 2
    quarter = HALF // 2
    pairs = (
        (owner_hbm, owner_row),
        (sizes_hbm, sizes),
        (occ_hbm, occ),
        (t_hbm.at[0], t_vmem),
    )
    copies = [
        pltpu.make_async_copy(source, here, in_sems.at[i])
        for i, (source, here) in enumerate(pairs)
    ]
    for copy in copies:
        copy.start()
    copies[0].wait()
    chip_row = owner_row[...] // 2
    first, second = iota((blocks, blocks), 0), iota((blocks, blocks), 1)
    chip_col = jnp.sum(jnp.where(first == second, chip_row, 0), axis=1, keepdims=True)
    same = chip_col == chip_row
    before = jnp.where(same & (first < second), 1.0, 0.0).astype(BF16)
    same = jnp.where(same, 1.0, 0.0).astype(BF16)
    for copy in copies[1:3]:
        copy.wait()
    wanted = pair[0] ^ occ[lax.axis_index("vir")]
    row = iota((8, blocks), 0)
    wide_all = wide_block(iota((1, blocks), 1), row, sizes)
    own = jnp.sum(jnp.where(row == wanted, wide_all, 0), axis=0, keepdims=True)
    rest = jnp.where(row == 0, own, jnp.where(row == 1, 1, 0))
    tallies = jnp.concatenate([wide_all, rest], axis=0).astype(F32).astype(BF16)
    ahead = jnp.dot(tallies, before, preferred_element_type=F32).astype(I32)
    total = jnp.dot(tallies, same, preferred_element_type=F32).astype(I32)
    owned = total[9:10]

    index = jnp.int32(0)
    if len(classes) > 1:
        used = jnp.int32(0)
        for m in range(occ.shape[0]):
            used = used | (jnp.int32(1) << (pair[0] ^ occ[m]))
        need = slots_needed(total[:8], owned) * ((used >> row) & 1)
        need = jnp.max(need) * BS
        for size in classes[:-1]:
            index = index + (need > size).astype(I32)
    choice[0] = index

    step = ALIGN // BS
    chip = iota((chips, 1), 0)
    lengths = jnp.where(chip == chip_row, slots_needed(total[8:9], owned), 0)
    lengths = (jnp.max(lengths, axis=1, keepdims=True) + (step - 1)) // step
    starts_row = jnp.sum(jnp.where(chip < chip_row, lengths, 0), axis=0, keepdims=True)
    starts = [jnp.sum(jnp.where(chip < q, lengths, 0)) for q in range(chips)]
    slot, kind = slots_of(own, ahead[9:10], ahead[8:9], total[8:9])
    place = starts_row * step + slot
    targets = [jnp.where(kind == 2, -1, place), jnp.where(kind == 1, -1, place)]

    partner = irrep_of(iota((virtuals, 1), 0), sizes) ^ wanted
    partner = jnp.broadcast_to(partner, (virtuals, HALF)).astype(I16)
    label_a = irrep_of(iota((1, virtuals), 1), sizes).astype(I16)
    copies[3].wait()
    halves = [jnp.zeros((virtuals, HALF), BF16) for _ in range(2)]
    for i, k in enumerate(range(0, virtuals, HALF)):
        here = partner == label_a[:, k : k + HALF]
        kept = jnp.where(here, t_vmem[:, k : k + HALF], jnp.zeros((), BF16))
        halves[i % 2] = halves[i % 2] + kept
    for h in range(2):
        folds[h] = halves[h].astype(F32)
    first, second = iota((blocks, blocks), 0), iota((blocks, blocks), 1)
    narrow = jnp.sum(jnp.where(first == second, own, 0), axis=1, keepdims=True) == 0
    blank = jnp.zeros((blocks, quarter), F32)
    sources = [[[], []], [[], []]]
    for r in range(BS):
        both = [folds[h, pl.ds(r, blocks, stride=BS), :] for h in range(2)]
        for h in range(2):
            source = both[h] + jnp.where(narrow, both[1 - h], 0.0)
            if rows_out < quarter:
                old, new = iota((HALF, HALF), 0), iota((HALF, HALF), 1)
                core, x = new // quarter, new % quarter
                lane = x // rows_out * (2 * rows_out) + core * rows_out + x % rows_out
                order = jnp.where(old == lane, 1.0, 0.0).astype(BF16)
                source = jnp.dot(source.astype(BF16), order, preferred_element_type=F32)
            for core in range(2):
                side = source[:, core * quarter : (core + 1) * quarter]
                sources[core][h] += [blank, side] if h else [side, blank]
    count = filled.shape[1] // BS
    slot = iota((count, 1), 0)
    hot = jnp.concatenate([jnp.where(x == slot, 1.0, 0.0) for x in targets], axis=1).astype(BF16)

    def send(k, device):
        start = pl.multiple_of(starts[device // 2] * ALIGN, ALIGN)
        return pltpu.make_async_copy(
            out.at[device % 2, pl.ds(start, classes[k])],
            outs[k].at[device],
            out_sems.at[device],
        )

    def each(core, act):
        for k in range(len(classes)):

            @pl.when(index == k)
            def _(k=k):
                for device in range(core, 2 * chips, 2):
                    act(send(k, device))

    for core in range(2):
        source = [jnp.concatenate(x, axis=1) for x in sources[core]]
        source = jnp.concatenate(source, axis=0).astype(BF16)
        moved = jnp.dot(hot, source, preferred_element_type=F32)
        for r in range(BS):
            part = slice(r * HALF, (r + 1) * HALF)
            filled[core, pl.ds(r, count, stride=BS), :] = moved[:, part]
        out[core, : filled.shape[1]] = filled[core].astype(BF16)
        rest = out.shape[1] - filled.shape[1]
        out[core, filled.shape[1] :] = jnp.zeros((rest, HALF), BF16)
        each(core, lambda copy: copy.start())
    for core in range(2):
        each(core, lambda copy: copy.wait())


def label_kernel(
    rows,
    rows_out,
    sizes,
    occ,
    pair,
    j_irrep,
    owner_row,
    label_row,
    label_k,
    slots,
    kinds,
    label_kept,
    label_out,
    keys,
):
    here = lax.axis_index("vir")
    occupied, lanes = label_k.shape
    virtuals = owner_row.shape[1] * BS
    target = virtual_place(block_place(owner_row[...], rows), virtuals)
    lane = iota((virtuals, lanes), 1)
    source = jnp.where(lane < rows, lane + here * rows, lane - rows + (here ^ 1) * rows)
    virtual = iota((virtuals, lanes), 0)
    e_row = jnp.sum(jnp.where(target == source, virtual + 1, 0), axis=0, keepdims=True) - 1
    label = irrep_of(e_row, sizes)
    label_row[...] = label[:, :rows]
    m_row = iota((occupied, 1), 0)
    wanted = jnp.zeros((occupied, 1), I32)
    for m in range(occupied):
        wanted = jnp.where(m_row == m, pair[0] ^ occ[m], wanted)
    partner = label ^ wanted
    label_k[...] = partner
    first, second = iota((lanes, lanes), 0), iota((lanes, lanes), 1)
    e_col = jnp.sum(jnp.where(first == second, e_row, 0), axis=1, keepdims=True)
    ahead = (e_col >= 0) & (e_col % BS == 0) & (e_col // BS < e_row // BS)
    wide = jnp.where(e_row >= 0, wide_block(jnp.maximum(e_row, 0) // BS, wanted, sizes), 0)
    rank_wide = jnp.dot(
        wide.astype(F32).astype(BF16),
        jnp.where(ahead, 1.0, 0.0).astype(BF16),
        preferred_element_type=F32,
    ).astype(I32)
    rank = jnp.sum(ahead.astype(I32), axis=0, keepdims=True)
    count_wide = jnp.sum(wide, axis=1, keepdims=True) // BS
    slot, kind = slots_of(wide, rank, rank_wide, count_wide)
    slots[...] = jnp.where(e_row >= 0, slot * BS + e_row % BS, -1)
    kinds[...] = kind
    row = iota(label_kept.shape, 0)
    a = row // rows_out * (2 * rows_out) + here % 2 * rows_out + row % rows_out
    label_kept[...] = irrep_of(a, sizes)
    label_out[...] = irrep_of(iota(label_out.shape, 0) + here * rows_out, sizes) ^ pair[0]
    keys[...] = jnp.broadcast_to(column_keys(keys.shape[1], sizes, j_irrep), keys.shape)


def fold_kernel(first, occ, label_row, keys, w, out, folded):
    step, part = pl.program_id(0), pl.program_id(1)
    row_block, m_block, columns = w.shape
    wide = out.shape[2]
    m_row = iota((m_block, 1), 0)
    occ_col = jnp.zeros((m_block, 1), I32)
    for i in range(m_block):
        occ_col = jnp.where(m_row == i, occ[part * m_block + i], occ_col)

    @pl.loop(0, row_block // 4)
    def _(quad):
        for i in range(4):
            row = quad * 4 + i
            label = label_row[first + step * row_block + row]
            allowed = (occ_col ^ label) == keys[:1, :]
            kept = jnp.where(allowed, w[row].astype(F32), 0.0)
            total = kept[:, :wide]
            for k in range(1, columns // wide):
                total = total + kept[:, k * wide : (k + 1) * wide]
            here = pl.ds(pl.multiple_of(row * m_block, m_block), m_block)
            for k in range(wide // 128):
                folded[k, here, :] = total[:, k * 128 : (k + 1) * 128]

    for i in range(m_block):
        for k in range(wide // 128):
            out[i, :, k * 128 : (k + 1) * 128] = folded[
                k, pl.ds(i, row_block, stride=m_block), :
            ].astype(BF16)


def product_kernel(pieces, label_k, slots, kinds, label_kept, packed, *refs):
    own, mate_hbm = refs[:pieces], refs[pieces : 2 * pieces]
    coded, out, t, mate, sems = refs[2 * pieces :]
    occupied, half, lanes = t.shape
    rows = lanes // 2
    kept = out.shape[0]
    size = rows // pieces
    copies = [
        pltpu.make_async_copy(mate_hbm[i], mate.at[:, i * size : (i + 1) * size], sems.at[i])
        for i in range(pieces)
    ]
    for copy in copies:
        copy.start()
    slot = iota((packed.shape[1], 1), 0)
    unpacked = max(1, min(occupied, 8))

    @pl.loop(0, occupied // unpacked)
    def _(step):
        for i in range(unpacked):
            m = step * unpacked + i
            hot = jnp.where(slots[pl.ds(m, 1), :] == slot, 1.0, 0.0).astype(BF16)
            both = lax.dot_general(
                packed[m], hot, (((0,), (0,)), ((), ())), preferred_element_type=F32
            )
            low, high = both[: half // 2], both[half // 2 :]
            kind = kinds[pl.ds(m, 1), :]
            t[m] = jnp.concatenate(
                [jnp.where(kind == 2, high, low), jnp.where(kind == 1, low, high)], axis=0
            ).astype(BF16)

    wide_label = jnp.broadcast_to(label_kept[:, :1], (kept, rows))

    def expand(m, side):
        lane = slice(side * rows, (side + 1) * rows)
        wanted = label_k[pl.ds(m, 1), :][:, lane]
        values = t[m][:, lane].astype(F32)
        return jnp.concatenate(
            [
                jnp.where(wide_label[k : k + half] == wanted, values, 0.0).astype(BF16)
                for k in range(0, kept, half)
            ],
            axis=0,
        )

    def couplings(m, side):
        return mate[m] if side else jnp.concatenate([piece[m] for piece in own], axis=0)

    def arrived(side):
        for copy in copies if side else ():
            copy.wait()

    if rows % 128 == 0:
        for side in range(2):
            arrived(side)
            left = jnp.concatenate([expand(m, side) for m in range(occupied)], axis=1)
            right = jnp.concatenate([couplings(m, side) for m in range(occupied)], axis=0)
            total = jnp.dot(left, right, preferred_element_type=F32)
            out[...] = out[...] + total if side else total
    else:
        arrived(1)
        out[...] = jnp.zeros(out.shape, F32)

        @pl.loop(0, occupied)
        def _(m):
            for side in range(2):
                out[...] += jnp.dot(
                    expand(m, side), couplings(m, side), preferred_element_type=F32
                )

    rows_out = kept // coded.shape[0]
    for chip in range(coded.shape[0]):
        coded[chip] = encode(out[chip * rows_out : (chip + 1) * rows_out, :])


def encode(values):
    row = iota((PAD, 128), 0)
    scales = jnp.zeros((PAD, 128), I32)
    blocks = []
    for i in range(values.shape[1] // 128):
        part = values[:, i * 128 : (i + 1) * 128]
        largest = jnp.maximum(jnp.max(jnp.abs(part), axis=0, keepdims=True), SMALL)
        scale = jnp.floor(jnp.log2(largest) * STEPS) + 2.0
        factor = jnp.exp2(scale * (-0.5 / STEPS))
        blocks.append(jnp.floor(part * factor * (factor * TOP) + 0.5).astype(I32))
        scales = jnp.where(row == i, scale.astype(I32), scales)
    return jnp.concatenate(blocks + [scales], axis=0).astype(I16)


def decode(coded, rows_out):
    values = coded.astype(I32)
    blocks = []
    for i in range((coded.shape[0] - PAD) // rows_out):
        scale = values[coded.shape[0] - PAD + i :][:1].astype(F32)
        factor = jnp.exp2(scale * (0.5 / STEPS))
        part = values[i * rows_out : (i + 1) * rows_out].astype(F32)
        blocks.append(part * (factor * (1.0 / TOP)) * factor)
    return blocks


def finish_kernel(label_out, keys, parts, out):
    chips = parts.shape[0]
    rows_out = out.shape[0]
    total = decode(parts[0], rows_out)
    for q in range(1, chips):
        total = [x + y for x, y in zip(total, decode(parts[q], rows_out))]
    total = jnp.concatenate(total, axis=1)
    wide = total.shape[1]
    for k in range(0, out.shape[1], wide):
        out[:, k : k + wide] = jnp.where(
            label_out[:, :1] == keys[:1, k : k + wide], total, 0.0
        )


in_hbm = functools.partial(pltpu.with_memory_space_constraint, memory_space=pltpu.HBM)
in_vmem = functools.partial(pltpu.with_memory_space_constraint, memory_space=pltpu.VMEM)


def per_device(amplitudes, couplings, occ_irrep, pair_irrep, j_irrep, block_sizes, owner):
    devices = lax.axis_size("vir")
    chips = devices // 2
    virtuals = amplitudes.shape[2]
    rows, occupied, columns = couplings.shape
    wide = columns // virtuals * MOST
    rows_out = virtuals // devices
    kept = virtuals // 2
    lanes = 2 * rows
    blocks = owner.shape[0]
    smem = pl.BlockSpec(memory_space=pltpu.SMEM)
    vmem = pl.BlockSpec(memory_space=pltpu.VMEM)
    hbm = pl.BlockSpec(memory_space=pltpu.HBM)
    params = pltpu.CompilerParams(vmem_limit_bytes=LIMIT)

    classes = [lanes]
    if lanes % 256 == 0:
        classes = [lanes // 16 * part for part in (11, 12, 13, 14, 16)]
    owner_row = owner.reshape(1, blocks)
    *outgoing, choice = pl.pallas_call(
        functools.partial(pack_kernel, rows_out, classes),
        out_shape=[jax.ShapeDtypeStruct((devices, size, HALF), BF16) for size in classes]
        + [jax.ShapeDtypeStruct((1,), I32)],
        in_specs=[hbm, hbm, smem, hbm, hbm],
        out_specs=[hbm] * len(classes) + [smem],
        scratch_shapes=[
            pltpu.SMEM(block_sizes.shape, I32),
            pltpu.SMEM(occ_irrep.shape, I32),
            pltpu.VMEM((1, blocks), I32),
            pltpu.VMEM((virtuals, virtuals), BF16),
            pltpu.VMEM((2, virtuals, HALF), F32),
            pltpu.VMEM((2, virtuals + chips * ALIGN, HALF), F32),
            pltpu.VMEM((2, virtuals + chips * ALIGN + lanes, HALF), BF16),
            pltpu.SemaphoreType.DMA((4,)),
            pltpu.SemaphoreType.DMA((devices,)),
        ],
        compiler_params=params,
        name="pack_amplitudes",
    )(
        in_hbm(block_sizes),
        in_hbm(occ_irrep),
        pair_irrep,
        in_hbm(owner_row),
        in_hbm(amplitudes),
    )

    def contract(packed):
        received = lax.all_to_all(packed, "vir", 0, 0)

        label_row, label_k, slots, kinds, label_kept, label_out, keys = pl.pallas_call(
            functools.partial(label_kernel, rows, rows_out),
            out_shape=(
                jax.ShapeDtypeStruct((1, rows), I32),
                jax.ShapeDtypeStruct((occupied, lanes), I32),
                jax.ShapeDtypeStruct((occupied, lanes), I32),
                jax.ShapeDtypeStruct((occupied, lanes), I32),
                jax.ShapeDtypeStruct((kept, 128), I32),
                jax.ShapeDtypeStruct((rows_out, 128), I32),
                jax.ShapeDtypeStruct((8, columns), I32),
            ),
            in_specs=[smem] * 4 + [vmem],
            out_specs=(vmem,) * 7,
            compiler_params=params,
            name="labels",
        )(block_sizes, occ_irrep, pair_irrep, j_irrep, owner_row)

        row_block, m_block = 16, 16
        pieces = max(1, rows // 32)
        piece_rows = rows // pieces
        w_own, w_mate = [], []
        for piece in range(pieces):
            first = piece * piece_rows
            w_own.append(
                pl.pallas_call(
                    functools.partial(fold_kernel, first),
                    out_shape=jax.ShapeDtypeStruct((occupied, piece_rows, wide), BF16),
                    grid=(piece_rows // row_block, occupied // m_block),
                    in_specs=[smem, smem, vmem]
                    + [
                        pl.BlockSpec(
                            (row_block, m_block, columns),
                            lambda i, j, skip=first // row_block: (skip + i, j, 0),
                        )
                    ],
                    out_specs=pl.BlockSpec((m_block, row_block, wide), lambda i, j: (j, i, 0)),
                    scratch_shapes=[pltpu.VMEM((wide // 128, row_block * m_block, 128), F32)],
                    compiler_params=params,
                    cost_estimate=pl.CostEstimate(
                        flops=4 * piece_rows * occupied * columns,
                        bytes_accessed=3 * piece_rows * occupied * columns,
                        transcendentals=0,
                    ),
                    name="fold_couplings",
                )(occ_irrep, label_row.reshape(rows), keys, in_hbm(couplings))
            )
            w_mate.append(lax.ppermute(w_own[-1], "vir", [(d, d ^ 1) for d in range(devices)]))

        partial = pl.pallas_call(
            functools.partial(product_kernel, pieces),
            out_shape=jax.ShapeDtypeStruct((chips, wide // 128 * rows_out + PAD, 128), I16),
            in_specs=[vmem] * (5 + pieces) + [hbm] * pieces,
            out_specs=vmem,
            scratch_shapes=[
                pltpu.VMEM((kept, wide), F32),
                pltpu.VMEM((occupied, HALF, lanes), BF16),
                pltpu.VMEM((occupied, rows, wide), BF16),
                pltpu.SemaphoreType.DMA((pieces,)),
            ],
            compiler_params=params,
            name="multiply",
        )(
            *[in_vmem(x) for x in (label_k, slots, kinds, label_kept, received, *w_own)],
            *[in_hbm(x) for x in w_mate],
        )
        sides = [[d for d in range(devices) if d % 2 == core] for core in (0, 1)]
        parts = lax.all_to_all(partial, "vir", 0, 0, axis_index_groups=sides)
        return pl.pallas_call(
            finish_kernel,
            out_shape=pltpu.HBM((rows_out, columns), F32),
            in_specs=[vmem] * 3,
            out_specs=vmem,
            compiler_params=params,
            name="unfold",
        )(label_out, keys, parts)

    if len(classes) == 1:
        return contract(outgoing[0])
    branches = [lambda *packed, k=k: contract(packed[k]) for k in range(len(classes))]
    return lax.switch(choice[0], branches, *outgoing)


def solution(mesh):
    return jax.shard_map(
        per_device,
        mesh=mesh,
        in_specs=(
            P(("grp", "vir"), None, None),
            P(("grp", "vir"), None, None),
            P("grp"),
            P(),
            P(),
            P("grp"),
            P("grp", None),
        ),
        out_specs=P(("grp", "vir"), None),
        check_vma=False,
    )
```

profile of v0, /device:TPU:0, one launch (start us, length us, event | category | flops | bytes accessed | tf_op | source)
XLA Modules:
  0.0 56.5 jit_solution(3282191654696540914)
XLA Ops:
  0.7 4.4 %pack_amplitudes.1 = (bf16[16,176,128]{2,1,0:T(8,128)(2,1)}, bf16[16,192,128]{2,1,0:T(8,128)(2,1)}, bf16[16,208,128]{2,1,0:T(8,128)(2,1)}, bf16[16,224,128]{2,1,...) custom-call(s32[8]{0:T(128)} %sizes_hbm.1, s32[16]{0:T(128)} %occ_hbm.1, s32[1]{0:T(128)S(6)} %copy.18.pair, ...), custom_call_target="tpu_custom_call" | custom-call | tf_op jit(solution)/shard_map/pack_amplitudes/pallas_call | solution.py:435
  5.7 50.8 %conditional.1 = (f32[64,2048]{1,0:T(8,128)}) conditional(s32[]{:T(128)} %bitcast.6, (s32[8]{0:T(128)}, s32[16]{0:T(128)}, s32[1]{0:T(128)}, s32[2]{0:T(128)}, s32[1,256]{1,0:T(1,128)}, /*index=5*/bf16[16,176,128]{2,1,0:T(8,128)(2,1)}, bf16[128,16,2048]{2,1,0:T(8,128)(2,1)}) %tuple.35, (s32[8]{0:T(128)}, ...), branch_computations={%region_0.0_spmd, %region_1.0_spmd, %region_2.0_spmd, %region_3.0_... | conditional | flops 16777216 | bytes 31523668 | solution.py:544
  5.7 0.0 copy-start.15
  5.7 7.4 %all-to-all-start = ((bf16[16,176,128]{2,1,0:T(8,128)(2,1)}), bf16[16,176,128]{2,1,0:T(8,128)(2,1)S(1)}, u32[]{:S(2)}, u32[]{:S(2)}) async-start(bf16[16,176,128]{2,1,0:T(8,128)(2,1)} %get-tuple-element.92), calls=%async_computation | async-start | bytes 1441792 | tf_op jit(solution)/shard_map/cond/branch_0_fun/all_to_all | solution.py:463
  13.1 2.4 %labels.5 = (s32[1,128]{1,0:T(1,128)S(1)}, s32[16,256]{1,0:T(8,128)S(1)}, s32[16,256]{1,0:T(8,128)S(1)}, s32[16,256]{1,0:T(8,128)S(1)}, s32[512,128]{1,0:T(8,128...) custom-call(s32[8]{0:T(128)} %get-tuple-element.70.sizes, s32[16]{0:T(128)} %get-tuple-element.80.occ, ...), custom_call_target="tpu_custom_call" | custom-call | tf_op jit(solution)/shard_map/cond/branch_0_fun/labels/pallas_call | solution.py:465
  15.6 2.3 %fold_couplings.20.refs_0_ = bf16[16,32,512]{2,1,0:T(8,128)(2,1)S(1)} custom-call(s32[16]{0:T(128)} %get-tuple-element.80.occ, s32[128]{0:T(128)S(1)} %bitcast.7, s32[8,2048]{1,0:T(8,128)S(1)} %get-tuple-element.87.keys, bf16[128,16,2048]{2,1,0:T(8,128)(2,1)} %get-tuple-element.94.w), custom_call_target="tpu_custom_call" | custom-call | flops 4194304 | bytes 3145728 | tf_op jit(solution)/shard_map/cond/branch_0_fun/fold_couplings/pallas_call | solution.py:489
  17.9 0.5 collective-permute-start
  18.3 0.0 copy-done.15
  18.3 2.3 %fold_couplings.21.refs_1_ = bf16[16,32,512]{2,1,0:T(8,128)(2,1)S(1)} custom-call(s32[16]{0:T(128)S(1)} %copy-done.15, s32[128]{0:T(128)S(1)} %bitcast.8, s32[8,2048]{1,0:T(8,128)S(1)} %get-tuple-element.87.keys, bf16[128,16,2048]{2,1,0:T(8,128)(2,1)} %get-tuple-element.94.w), custom_call_target="tpu_custom_call" | custom-call | flops 4194304 | bytes 3145728 | tf_op jit(solution)/shard_map/cond/branch_0_fun/fold_couplings/pallas_call | solution.py:489
  20.7 0.2 collective-permute-start.1
  20.8 2.3 %fold_couplings.22.refs_2_ = bf16[16,32,512]{2,1,0:T(8,128)(2,1)S(1)} custom-call(s32[16]{0:T(128)S(1)} %copy-done.15, s32[128]{0:T(128)S(1)} %bitcast.9, s32[8,2048]{1,0:T(8,128)S(1)} %get-tuple-element.87.keys, bf16[128,16,2048]{2,1,0:T(8,128)(2,1)} %get-tuple-element.94.w), custom_call_target="tpu_custom_call" | custom-call | flops 4194304 | bytes 3145728 | tf_op jit(solution)/shard_map/cond/branch_0_fun/fold_couplings/pallas_call | solution.py:489
  23.1 0.5 collective-permute-start.2
  23.6 2.3 %fold_couplings.23.refs_3_ = bf16[16,32,512]{2,1,0:T(8,128)(2,1)S(1)} custom-call(s32[16]{0:T(128)S(1)} %copy-done.15, s32[128]{0:T(128)S(1)} %bitcast.10, s32[8,2048]{1,0:T(8,128)S(1)} %get-tuple-element.87.keys, bf16[128,16,2048]{2,1,0:T(8,128)(2,1)} %get-tuple-element.94.w), custom_call_target="tpu_custom_call" | custom-call | flops 4194304 | bytes 3145728 | tf_op jit(solution)/shard_map/cond/branch_0_fun/fold_couplings/pallas_call | solution.py:489
  25.9 0.2 collective-permute-start.3
  26.1 0.0 collective-permute-done.refs_4_
  26.1 0.0 copy-start.12
  26.1 0.0 collective-permute-done.1.refs_5_
  26.1 0.0 copy-start.13
  26.1 0.0 collective-permute-done.2.refs_6_
  26.1 0.8 %copy-done.12 = bf16[16,32,512]{2,1,0:T(8,128)(2,1)} copy-done((bf16[16,32,512]{2,1,0:T(8,128)(2,1)}, bf16[16,32,512]{2,1,0:T(8,128)(2,1)S(1)}, u32[]{:S(2)}) %copy-start.12) | copy-done | bytes 524312 | tf_op jit(solution)/shard_map/cond
  26.9 0.2 copy-done.13
  27.1 0.0 copy-start.14
  27.1 0.8 %copy-done.14 = bf16[16,32,512]{2,1,0:T(8,128)(2,1)} copy-done((bf16[16,32,512]{2,1,0:T(8,128)(2,1)}, bf16[16,32,512]{2,1,0:T(8,128)(2,1)S(1)}, u32[]{:S(2)}) %copy-start.14) | copy-done | bytes 524312 | tf_op jit(solution)/shard_map/cond
  27.9 0.2 collective-permute-done.3.refs_7_
  28.0 2.8 %all-to-all-done.packed = bf16[16,176,128]{2,1,0:T(8,128)(2,1)S(1)} async-done(((bf16[16,176,128]{2,1,0:T(8,128)(2,1)}), bf16[16,176,128]{2,1,0:T(8,128)(2,1)S(1)}, u32[]{:S(2)}, u32[]{:S(2)}) %all-to-all-start) | async-done | bytes 720928 | tf_op jit(solution)/shard_map/cond/branch_0_fun/all_to_all | solution.py:463
  30.8 3.4 %multiply.5 = s16[8,272,128]{2,1,0:T(8,128)(2,1)S(1)} custom-call(s32[16,256]{1,0:T(8,128)S(1)} %get-tuple-element.88.label_k, s32[16,256]{1,0:T(8,128)S(1)} %get-tuple-element.89.slots, s32[16,256]{1,0:T(8,128)S(1)} %get-tuple-element.90.kinds, s32[512,128]{1,0:T(8,128)S(1)} %get-tuple-element.91.label_kept, bf16[16,176,128]{2,1,0:T(8,128)(2,1)S(1)} %all-to-all-done.packed, ...), custom_call_target="tpu_custom_call" | custom-call | tf_op jit(solution)/shard_map/cond/branch_0_fun/multiply/pallas_call | solution.py:513
  34.2 21.2 %all_to_all.40.parts = s16[8,272,128]{2,1,0:T(8,128)(2,1)S(1)} all-to-all(s16[8,272,128]{2,1,0:T(8,128)(2,1)S(1)} %multiply.5), channel_id=1, replica_groups={{0,2,4,6,8,10,12,14},{1,3,5,7,9,11,13,15},{16,18,20,22,24,26,28,30},{17..., dimensions={0} | all-to-all | bytes 1114112 | tf_op jit(solution)/shard_map/cond/branch_0_fun/all_to_all | solution.py:531
  55.5 1.0 %unfold.5 = f32[64,2048]{1,0:T(8,128)} custom-call(s32[64,128]{1,0:T(8,128)S(1)} %get-tuple-element.86.label_out, s32[8,2048]{1,0:T(8,128)S(1)} %get-tuple-element.87.keys, s16[8,272,128]{2,1,0:T(8,128)(2,1)S(1)} %all_to_all.40.parts), custom_call_target="tpu_custom_call" | custom-call | tf_op jit(solution)/shard_map/cond/branch_0_fun/unfold/pallas_call | solution.py:532
Async XLA Ops:
  5.7 12.6 %copy-start.15 = (s32[16]{0:T(128)S(1)}, s32[16]{0:T(128)}, u32[]{:S(2)}) copy-start(s32[16]{0:T(128)} %get-tuple-element.80.occ) | copy-start | bytes 196 | tf_op jit(solution)/shard_map/cond
  5.7 25.1 %all-to-all-start = ((bf16[16,176,128]{2,1,0:T(8,128)(2,1)}), bf16[16,176,128]{2,1,0:T(8,128)(2,1)S(1)}, u32[]{:S(2)}, u32[]{:S(2)}) async-start(bf16[16,176,128]{2,1,0:T(8,128)(2,1)} %get-tuple-element.92), calls=%async_computation | async-start | bytes 1441792 | tf_op jit(solution)/shard_map/cond/branch_0_fun/all_to_all | solution.py:463
  17.9 8.2 %collective-permute-start = (bf16[16,32,512]{2,1,0:T(8,128)(2,1)S(1)}, bf16[16,32,512]{2,1,0:T(8,128)(2,1)S(1)}, u32[]{:S(2)}, u32[]{:S(2)}) collective-permute-start(bf16[16,32,512]{2,1,0:T(8,128)(2,1)S(1)} %fold_couplings.20.refs_0_), channel_id=1, source_target_pairs={{0,1},{1,0},{2,3},{3,2},{4,5},{5,4},{6,7},{7,6},{8,9},{9,8},{10,11... | collective-permute-start | bytes 1572872 | tf_op jit(solution)/shard_map/cond/branch_0_fun/ppermute | solution.py:511
  20.7 5.4 %collective-permute-start.1 = (bf16[16,32,512]{2,1,0:T(8,128)(2,1)S(1)}, bf16[16,32,512]{2,1,0:T(8,128)(2,1)S(1)}, u32[]{:S(2)}, u32[]{:S(2)}) collective-permute-start(bf16[16,32,512]{2,1,0:T(8,128)(2,1)S(1)} %fold_couplings.21.refs_1_), channel_id=1, source_target_pairs={{0,1},{1,0},{2,3},{3,2},{4,5},{5,4},{6,7},{7,6},{8,9},{9,8},{10,11... | collective-permute-start | bytes 1572872 | tf_op jit(solution)/shard_map/cond/branch_0_fun/ppermute | solution.py:511
  23.1 3.0 %collective-permute-start.2 = (bf16[16,32,512]{2,1,0:T(8,128)(2,1)S(1)}, bf16[16,32,512]{2,1,0:T(8,128)(2,1)S(1)}, u32[]{:S(2)}, u32[]{:S(2)}) collective-permute-start(bf16[16,32,512]{2,1,0:T(8,128)(2,1)S(1)} %fold_couplings.22.refs_2_), channel_id=1, source_target_pairs={{0,1},{1,0},{2,3},{3,2},{4,5},{5,4},{6,7},{7,6},{8,9},{9,8},{10,11... | collective-permute-start | bytes 1572872 | tf_op jit(solution)/shard_map/cond/branch_0_fun/ppermute | solution.py:511
  25.9 2.1 %collective-permute-start.3 = (bf16[16,32,512]{2,1,0:T(8,128)(2,1)S(1)}, bf16[16,32,512]{2,1,0:T(8,128)(2,1)}, u32[]{:S(2)}, u32[]{:S(2)}) collective-permute-start(bf16[16,32,512]{2,1,0:T(8,128)(2,1)S(1)} %fold_couplings.23.refs_3_), channel_id=1, source_target_pairs={{0,1},{1,0},{2,3},{3,2},{4,5},{5,4},{6,7},{7,6},{8,9},{9,8},{10,11... | collective-permute-start | bytes 1572872 | tf_op jit(solution)/shard_map/cond/branch_0_fun/ppermute | solution.py:511
  26.1 0.8 %copy-start.12 = (bf16[16,32,512]{2,1,0:T(8,128)(2,1)}, bf16[16,32,512]{2,1,0:T(8,128)(2,1)S(1)}, u32[]{:S(2)}) copy-start(bf16[16,32,512]{2,1,0:T(8,128)(2,1)S(1)} %collective-permute-done.refs_4_) | copy-start | bytes 1572868 | tf_op jit(solution)/shard_map/cond
  26.1 1.0 %copy-start.13 = (bf16[16,32,512]{2,1,0:T(8,128)(2,1)}, bf16[16,32,512]{2,1,0:T(8,128)(2,1)S(1)}, u32[]{:S(2)}) copy-start(bf16[16,32,512]{2,1,0:T(8,128)(2,1)S(1)} %collective-permute-done.1.refs_5_) | copy-start | bytes 1572868 | tf_op jit(solution)/shard_map/cond
  27.1 0.8 %copy-start.14 = (bf16[16,32,512]{2,1,0:T(8,128)(2,1)}, bf16[16,32,512]{2,1,0:T(8,128)(2,1)S(1)}, u32[]{:S(2)}) copy-start(bf16[16,32,512]{2,1,0:T(8,128)(2,1)S(1)} %collective-permute-done.2.refs_6_) | copy-start | bytes 1572868 | tf_op jit(solution)/shard_map/cond
where the time goes:
time: 56.9 us; the launch traced here: 56.5 us
  blocking collectives  21.2 us (37%)
  Pallas kernels  20.5 us (36%)
  starting transfers between devices  8.68 us (15%)
  waiting for transfers between devices  2.93 us (5%)
  local copies, waits for them, and re-layouts  1.75 us (3%)
  between operations  1.31 us (2%)
    all_to_all x1, blocking collectives, contract(): parts = lax.all_to_all(partial, 'vir', 0, 0, axis_index_groups=sides)  21.2 us
    pallas_call x4, Pallas kernels, contract(): pl.pallas_call(functools.partial(fold_kernel, first), out_shape=jax.Shape...  9.2 us
    all_to_all x1, starting transfers between devices, contract(): received = lax.all_to_all(packed, 'vir', 0, 0)  7.39 us
    pallas_call x1, Pallas kernels, per_device(): pl.pallas_call(functools.partial(pack_kernel, rows_out, classes), out_sha...  4.39 us
    pallas_call x1, Pallas kernels, contract(): pl.pallas_call(functools.partial(product_kernel, pieces), out_shape=jax.S...  3.42 us
    all_to_all x1, waiting for transfers between devices, contract(): received = lax.all_to_all(packed, 'vir', 0, 0)  2.76 us
    pallas_call x1, Pallas kernels, contract(): pl.pallas_call(functools.partial(label_kernel, rows, rows_out), out_shape...  2.44 us
    cond x8, local copies, waits for them, and re-layouts  1.75 us
  transfers between devices with their start and end apart: 5, of which 2 were waited for; matrix products, arithmetic and copies ran while one was open for 0% of the time, Pallas kernels for 21%

commit v1 on v0

--- a/solution.py
+++ b/solution.py
@@ -435,7 +435,7 @@
     *outgoing, choice = pl.pallas_call(
         functools.partial(pack_kernel, rows_out, classes),
         out_shape=[jax.ShapeDtypeStruct((devices, size, HALF), BF16) for size in classes]
-        + [jax.ShapeDtypeStruct((1,), I32)],
+        + [pltpu.SMEM((1,), I32)],
         in_specs=[hbm, hbm, smem, hbm, hbm],
         out_specs=[hbm] * len(classes) + [smem],
         scratch_shapes=[

time: 56.9 us -> 55.7 us (0.979)
  between operations: 1.31 us -> 0.67 us
  Pallas kernels: 20.5 us -> 19.9 us
where the time goes in v1:
time: 55.7 us; the launch traced here: 55.3 us
  blocking collectives  21.2 us (38%)
  Pallas kernels  19.9 us (36%)
  starting transfers between devices  8.68 us (16%)
  waiting for transfers between devices  2.93 us (5%)
  local copies, waits for them, and re-layouts  1.75 us (3%)
  between operations  0.67 us (1%)
    all_to_all x1, blocking collectives, contract(): parts = lax.all_to_all(partial, 'vir', 0, 0, axis_index_groups=sides)  21.2 us
    pallas_call x4, Pallas kernels, contract(): pl.pallas_call(functools.partial(fold_kernel, first), out_shape=jax.Shape...  9.2 us
    all_to_all x1, starting transfers between devices, contract(): received = lax.all_to_all(packed, 'vir', 0, 0)  7.39 us
    pallas_call x1, Pallas kernels, per_device(): pl.pallas_call(functools.partial(pack_kernel, rows_out, classes), out_sha...  3.87 us
    pallas_call x1, Pallas kernels, contract(): pl.pallas_call(functools.partial(product_kernel, pieces), out_shape=jax.S...  3.41 us
    all_to_all x1, waiting for transfers between devices, contract(): received = lax.all_to_all(packed, 'vir', 0, 0)  2.76 us
    pallas_call x1, Pallas kernels, contract(): pl.pallas_call(functools.partial(label_kernel, rows, rows_out), out_shape...  2.44 us
    cond x8, local copies, waits for them, and re-layouts  1.75 us
  transfers between devices with their start and end apart: 5, of which 2 were waited for; matrix products, arithmetic and copies ran while one was open for 0% of the time, Pallas kernels for 21%

profile of v1, /device:TPU:0, one launch (start us, length us, event | category | flops | bytes accessed | tf_op | source)
XLA Modules:
  0.0 55.3 jit_solution(13483818206093557977)
XLA Ops:
  0.7 3.9 %pack_amplitudes.1 = (bf16[16,176,128]{2,1,0:T(8,128)(2,1)}, bf16[16,192,128]{2,1,0:T(8,128)(2,1)}, bf16[16,208,128]{2,1,0:T(8,128)(2,1)}, bf16[16,224,128]{2,1,...) custom-call(s32[8]{0:T(128)} %sizes_hbm.1, s32[16]{0:T(128)} %occ_hbm.1, s32[1]{0:T(128)S(6)} %copy.18.pair, ...), custom_call_target="tpu_custom_call" | custom-call | tf_op jit(solution)/shard_map/pack_amplitudes/pallas_call | solution.py:435
  4.5 50.8 %conditional.1 = (f32[64,2048]{1,0:T(8,128)}) conditional(s32[]{:T(128)} %bitcast.6, (s32[8]{0:T(128)}, s32[16]{0:T(128)}, s32[1]{0:T(128)}, s32[2]{0:T(128)}, s32[1,256]{1,0:T(1,128)}, /*index=5*/bf16[16,176,128]{2,1,0:T(8,128)(2,1)}, bf16[128,16,2048]{2,1,0:T(8,128)(2,1)}) %tuple.35, (s32[8]{0:T(128)}, ...), branch_computations={%region_0.0_spmd, %region_1.0_spmd, %region_2.0_spmd, %region_3.0_... | conditional | flops 16777216 | bytes 31523668 | solution.py:544
  4.6 0.0 copy-start.15
  4.6 7.4 %all-to-all-start = ((bf16[16,176,128]{2,1,0:T(8,128)(2,1)}), bf16[16,176,128]{2,1,0:T(8,128)(2,1)S(1)}, u32[]{:S(2)}, u32[]{:S(2)}) async-start(bf16[16,176,128]{2,1,0:T(8,128)(2,1)} %get-tuple-element.92), calls=%async_computation | async-start | bytes 1441792 | tf_op jit(solution)/shard_map/cond/branch_0_fun/all_to_all | solution.py:463
  12.0 2.4 %labels.5 = (s32[1,128]{1,0:T(1,128)S(1)}, s32[16,256]{1,0:T(8,128)S(1)}, s32[16,256]{1,0:T(8,128)S(1)}, s32[16,256]{1,0:T(8,128)S(1)}, s32[512,128]{1,0:T(8,128...) custom-call(s32[8]{0:T(128)} %get-tuple-element.70.sizes, s32[16]{0:T(128)} %get-tuple-element.80.occ, ...), custom_call_target="tpu_custom_call" | custom-call | tf_op jit(solution)/shard_map/cond/branch_0_fun/labels/pallas_call | solution.py:465
  14.4 2.3 %fold_couplings.20.refs_0_ = bf16[16,32,512]{2,1,0:T(8,128)(2,1)S(1)} custom-call(s32[16]{0:T(128)} %get-tuple-element.80.occ, s32[128]{0:T(128)S(1)} %bitcast.7, s32[8,2048]{1,0:T(8,128)S(1)} %get-tuple-element.87.keys, bf16[128,16,2048]{2,1,0:T(8,128)(2,1)} %get-tuple-element.94.w), custom_call_target="tpu_custom_call" | custom-call | flops 4194304 | bytes 3145728 | tf_op jit(solution)/shard_map/cond/branch_0_fun/fold_couplings/pallas_call | solution.py:489
  16.7 0.5 collective-permute-start
  17.2 0.0 copy-done.15
  17.2 2.3 %fold_couplings.21.refs_1_ = bf16[16,32,512]{2,1,0:T(8,128)(2,1)S(1)} custom-call(s32[16]{0:T(128)S(1)} %copy-done.15, s32[128]{0:T(128)S(1)} %bitcast.8, s32[8,2048]{1,0:T(8,128)S(1)} %get-tuple-element.87.keys, bf16[128,16,2048]{2,1,0:T(8,128)(2,1)} %get-tuple-element.94.w), custom_call_target="tpu_custom_call" | custom-call | flops 4194304 | bytes 3145728 | tf_op jit(solution)/shard_map/cond/branch_0_fun/fold_couplings/pallas_call | solution.py:489
  19.5 0.2 collective-permute-start.1
  19.7 2.3 %fold_couplings.22.refs_2_ = bf16[16,32,512]{2,1,0:T(8,128)(2,1)S(1)} custom-call(s32[16]{0:T(128)S(1)} %copy-done.15, s32[128]{0:T(128)S(1)} %bitcast.9, s32[8,2048]{1,0:T(8,128)S(1)} %get-tuple-element.87.keys, bf16[128,16,2048]{2,1,0:T(8,128)(2,1)} %get-tuple-element.94.w), custom_call_target="tpu_custom_call" | custom-call | flops 4194304 | bytes 3145728 | tf_op jit(solution)/shard_map/cond/branch_0_fun/fold_couplings/pallas_call | solution.py:489
  22.0 0.5 collective-permute-start.2
  22.4 2.3 %fold_couplings.23.refs_3_ = bf16[16,32,512]{2,1,0:T(8,128)(2,1)S(1)} custom-call(s32[16]{0:T(128)S(1)} %copy-done.15, s32[128]{0:T(128)S(1)} %bitcast.10, s32[8,2048]{1,0:T(8,128)S(1)} %get-tuple-element.87.keys, bf16[128,16,2048]{2,1,0:T(8,128)(2,1)} %get-tuple-element.94.w), custom_call_target="tpu_custom_call" | custom-call | flops 4194304 | bytes 3145728 | tf_op jit(solution)/shard_map/cond/branch_0_fun/fold_couplings/pallas_call | solution.py:489
  24.8 0.2 collective-permute-start.3
  24.9 0.0 collective-permute-done.refs_4_
  24.9 0.0 copy-start.12
  24.9 0.0 collective-permute-done.1.refs_5_
  24.9 0.0 copy-start.13
  24.9 0.0 collective-permute-done.2.refs_6_
  25.0 0.8 %copy-done.12 = bf16[16,32,512]{2,1,0:T(8,128)(2,1)} copy-done((bf16[16,32,512]{2,1,0:T(8,128)(2,1)}, bf16[16,32,512]{2,1,0:T(8,128)(2,1)S(1)}, u32[]{:S(2)}) %copy-start.12) | copy-done | bytes 524312 | tf_op jit(solution)/shard_map/cond
  25.7 0.2 copy-done.13
  25.9 0.0 copy-start.14
  25.9 0.8 %copy-done.14 = bf16[16,32,512]{2,1,0:T(8,128)(2,1)} copy-done((bf16[16,32,512]{2,1,0:T(8,128)(2,1)}, bf16[16,32,512]{2,1,0:T(8,128)(2,1)S(1)}, u32[]{:S(2)}) %copy-start.14) | copy-done | bytes 524312 | tf_op jit(solution)/shard_map/cond
  26.7 0.2 collective-permute-done.3.refs_7_
  26.9 2.8 %all-to-all-done.packed = bf16[16,176,128]{2,1,0:T(8,128)(2,1)S(1)} async-done(((bf16[16,176,128]{2,1,0:T(8,128)(2,1)}), bf16[16,176,128]{2,1,0:T(8,128)(2,1)S(1)}, u32[]{:S(2)}, u32[]{:S(2)}) %all-to-all-start) | async-done | bytes 720928 | tf_op jit(solution)/shard_map/cond/branch_0_fun/all_to_all | solution.py:463
  29.6 3.4 %multiply.5 = s16[8,272,128]{2,1,0:T(8,128)(2,1)S(1)} custom-call(s32[16,256]{1,0:T(8,128)S(1)} %get-tuple-element.88.label_k, s32[16,256]{1,0:T(8,128)S(1)} %get-tuple-element.89.slots, s32[16,256]{1,0:T(8,128)S(1)} %get-tuple-element.90.kinds, s32[512,128]{1,0:T(8,128)S(1)} %get-tuple-element.91.label_kept, bf16[16,176,128]{2,1,0:T(8,128)(2,1)S(1)} %all-to-all-done.packed, ...), custom_call_target="tpu_custom_call" | custom-call | tf_op jit(solution)/shard_map/cond/branch_0_fun/multiply/pallas_call | solution.py:513
  33.0 21.2 %all_to_all.40.parts = s16[8,272,128]{2,1,0:T(8,128)(2,1)S(1)} all-to-all(s16[8,272,128]{2,1,0:T(8,128)(2,1)S(1)} %multiply.5), channel_id=1, replica_groups={{0,2,4,6,8,10,12,14},{1,3,5,7,9,11,13,15},{16,18,20,22,24,26,28,30},{17..., dimensions={0} | all-to-all | bytes 1114112 | tf_op jit(solution)/shard_map/cond/branch_0_fun/all_to_all | solution.py:531
  54.3 1.0 %unfold.5 = f32[64,2048]{1,0:T(8,128)} custom-call(s32[64,128]{1,0:T(8,128)S(1)} %get-tuple-element.86.label_out, s32[8,2048]{1,0:T(8,128)S(1)} %get-tuple-element.87.keys, s16[8,272,128]{2,1,0:T(8,128)(2,1)S(1)} %all_to_all.40.parts), custom_call_target="tpu_custom_call" | custom-call | tf_op jit(solution)/shard_map/cond/branch_0_fun/unfold/pallas_call | solution.py:532
Async XLA Ops:
  4.6 12.6 %copy-start.15 = (s32[16]{0:T(128)S(1)}, s32[16]{0:T(128)}, u32[]{:S(2)}) copy-start(s32[16]{0:T(128)} %get-tuple-element.80.occ) | copy-start | bytes 196 | tf_op jit(solution)/shard_map/cond
  4.6 25.1 %all-to-all-start = ((bf16[16,176,128]{2,1,0:T(8,128)(2,1)}), bf16[16,176,128]{2,1,0:T(8,128)(2,1)S(1)}, u32[]{:S(2)}, u32[]{:S(2)}) async-start(bf16[16,176,128]{2,1,0:T(8,128)(2,1)} %get-tuple-element.92), calls=%async_computation | async-start | bytes 1441792 | tf_op jit(solution)/shard_map/cond/branch_0_fun/all_to_all | solution.py:463
  16.7 8.2 %collective-permute-start = (bf16[16,32,512]{2,1,0:T(8,128)(2,1)S(1)}, bf16[16,32,512]{2,1,0:T(8,128)(2,1)S(1)}, u32[]{:S(2)}, u32[]{:S(2)}) collective-permute-start(bf16[16,32,512]{2,1,0:T(8,128)(2,1)S(1)} %fold_couplings.20.refs_0_), channel_id=1, source_target_pairs={{0,1},{1,0},{2,3},{3,2},{4,5},{5,4},{6,7},{7,6},{8,9},{9,8},{10,11... | collective-permute-start | bytes 1572872 | tf_op jit(solution)/shard_map/cond/branch_0_fun/ppermute | solution.py:511
  19.5 5.4 %collective-permute-start.1 = (bf16[16,32,512]{2,1,0:T(8,128)(2,1)S(1)}, bf16[16,32,512]{2,1,0:T(8,128)(2,1)S(1)}, u32[]{:S(2)}, u32[]{:S(2)}) collective-permute-start(bf16[16,32,512]{2,1,0:T(8,128)(2,1)S(1)} %fold_couplings.21.refs_1_), channel_id=1, source_target_pairs={{0,1},{1,0},{2,3},{3,2},{4,5},{5,4},{6,7},{7,6},{8,9},{9,8},{10,11... | collective-permute-start | bytes 1572872 | tf_op jit(solution)/shard_map/cond/branch_0_fun/ppermute | solution.py:511
  22.0 3.0 %collective-permute-start.2 = (bf16[16,32,512]{2,1,0:T(8,128)(2,1)S(1)}, bf16[16,32,512]{2,1,0:T(8,128)(2,1)S(1)}, u32[]{:S(2)}, u32[]{:S(2)}) collective-permute-start(bf16[16,32,512]{2,1,0:T(8,128)(2,1)S(1)} %fold_couplings.22.refs_2_), channel_id=1, source_target_pairs={{0,1},{1,0},{2,3},{3,2},{4,5},{5,4},{6,7},{7,6},{8,9},{9,8},{10,11... | collective-permute-start | bytes 1572872 | tf_op jit(solution)/shard_map/cond/branch_0_fun/ppermute | solution.py:511
  24.8 2.1 %collective-permute-start.3 = (bf16[16,32,512]{2,1,0:T(8,128)(2,1)S(1)}, bf16[16,32,512]{2,1,0:T(8,128)(2,1)}, u32[]{:S(2)}, u32[]{:S(2)}) collective-permute-start(bf16[16,32,512]{2,1,0:T(8,128)(2,1)S(1)} %fold_couplings.23.refs_3_), channel_id=1, source_target_pairs={{0,1},{1,0},{2,3},{3,2},{4,5},{5,4},{6,7},{7,6},{8,9},{9,8},{10,11... | collective-permute-start | bytes 1572872 | tf_op jit(solution)/shard_map/cond/branch_0_fun/ppermute | solution.py:511
  24.9 0.8 %copy-start.12 = (bf16[16,32,512]{2,1,0:T(8,128)(2,1)}, bf16[16,32,512]{2,1,0:T(8,128)(2,1)S(1)}, u32[]{:S(2)}) copy-start(bf16[16,32,512]{2,1,0:T(8,128)(2,1)S(1)} %collective-permute-done.refs_4_) | copy-start | bytes 1572868 | tf_op jit(solution)/shard_map/cond
  24.9 1.0 %copy-start.13 = (bf16[16,32,512]{2,1,0:T(8,128)(2,1)}, bf16[16,32,512]{2,1,0:T(8,128)(2,1)S(1)}, u32[]{:S(2)}) copy-start(bf16[16,32,512]{2,1,0:T(8,128)(2,1)S(1)} %collective-permute-done.1.refs_5_) | copy-start | bytes 1572868 | tf_op jit(solution)/shard_map/cond
  25.9 0.8 %copy-start.14 = (bf16[16,32,512]{2,1,0:T(8,128)(2,1)}, bf16[16,32,512]{2,1,0:T(8,128)(2,1)S(1)}, u32[]{:S(2)}) copy-start(bf16[16,32,512]{2,1,0:T(8,128)(2,1)S(1)} %collective-permute-done.2.refs_6_) | copy-start | bytes 1572868 | tf_op jit(solution)/shard_map/cond
